TPU v7x, 256 devices: a whole 4x4x8 slice. The times are simulated.
256 devices in a mesh: wave: 32 (over z, x_lo, core), rows: 8 (over y, x_hi).
Axes of the slice: x: 4 (x_hi: 2, x_lo: 2; x = x_hi * 2 + x_lo), y: 4, z: 8, core: 2. Of those that a mesh axis runs over, the one named last changes fastest.
Arguments:
- potential: bfloat16 [4, 512, 2048], P(None, 'rows', 'wave'), may hold values from 0 to 1
- tilt_index: int32 [64, 2], P('wave'), may hold values from -128 to 127
Outputs:
- exit_wave: bfloat16 [2, 64, 512, 2048], P(None, 'wave', 'rows')
All inputs are finite; a program needn't handle non-finite values.
Results may differ from a plain program's by a relative error of at most 0.025.
Values may be sent and summed in bfloat16 or wider, within the bound.
No kernel may reach another device: no remote copies, remote signals or barrier semaphores. Data moves between devices by JAX's collectives and lax.ppermute only.
A program may use at most 64 MiB of HBM per device.

v0:
```python
import functools
import math

import jax
import jax.numpy as jnp
import numpy as np
from jax import lax
from jax.experimental import pallas as pl
from jax.experimental.pallas import tpu as pltpu
from jax.sharding import PartitionSpec as P

NX = 2048
NY = 512
TAPS = 33
REACH = TAPS // 2
SLICES = 4
ROWS = 64
LANES = 128
BLOCKS = NX // LANES
ZS, WAVE, RANKS = 8, 32, 8
HALO = [REACH * (SLICES - s) for s in range(SLICES)]
IN_ROWS = [ROWS + 2 * h for h in HALO]
HALF = [n // 2 for n in IN_ROWS]
HALF_AT = [sum(HALF[:s]) for s in range(SLICES)]
HALF_ALL = sum(HALF)
BOTH = ("wave", "rows")
CORE_ROWS = ROWS // 2
HALO_ALL = sum(HALO)


def place(z, lo, core, rank):
    return ((z * 2 + lo) * 2 + core) * RANKS + rank


def send(value, target_of):
    pairs = []
    for z in range(ZS):
        for lo in range(2):
            for core in range(2):
                for rank in range(RANKS):
                    target = target_of(z, lo, core, rank)
                    if target is not None:
                        pairs.append((place(z, lo, core, rank), place(*target)))
    return lax.ppermute(value, BOTH, pairs)


def to_core(z, lo, core, rank):
    return z, lo, 1 - core, rank


def to_pair(z, lo, core, rank):
    return z, 1 - lo, core, rank


def to_rank(z, lo, core, rank):
    rank += 1 - 2 * core
    return (z, lo, core, rank) if 0 <= rank < RANKS else None


def to_next(z, lo, core, rank):
    return (z + 1 - 2 * core) % ZS, lo, core, rank


def taps():
    d = np.arange(TAPS, dtype=np.float32) - REACH
    angle = np.float32(math.pi) * d * d / TAPS
    scale = np.float32(1.0 / math.sqrt(TAPS))
    return np.cos(angle) * scale, np.sin(angle) * scale


def band(inside, outside, shift):
    at = np.arange(inside)[:, None] - np.arange(outside)[None, :] + shift
    valid = (at >= 0) & (at < TAPS)
    at = np.clip(at, 0, TAPS - 1)
    return tuple(np.where(valid, part[at], np.float32(0.0)) for part in taps())


def column_weights():
    def packed(re, im):
        return np.block([[re, im], [-im, re]])

    middle = band(LANES, LANES, REACH)
    left = band(LANES, LANES, REACH - LANES)
    right = band(LANES, LANES, REACH + LANES)
    return np.concatenate([packed(*middle), packed(left[0] + right[0], left[1] + right[1])])


def row_weights(s):
    re, im = (part.T for part in band(IN_ROWS[s], IN_ROWS[s] - 2 * REACH, 0))
    return np.block([[re, -im], [im, re]])


def polynomial(func, degree):
    w = 0.125 * (1.0 + np.cos(np.pi * (np.arange(64) + 0.5) / 64))
    fit = np.polynomial.chebyshev.Chebyshev.fit(w, func(3.0 * np.sqrt(w)), degree, domain=[0.0, 0.25])
    return [float(c) for c in fit.convert(kind=np.polynomial.Polynomial).coef]


EVEN = polynomial(np.cos, 4)
ODD = polynomial(lambda x: np.sin(x) / (x / 3.0), 4)


def horner(coefs, w):
    total = jnp.full_like(w, coefs[-1])
    for c in coefs[-2::-1]:
        total = total * w + c
    return total


def cosine_sine(tile):
    v = tile - 0.5
    w = v * v
    cos_v, sin_v = horner(EVEN, w), horner(ODD, w) * v
    c, s = math.cos(1.5), math.sin(1.5)
    return cos_v * c - sin_v * s, cos_v * s + sin_v * c


ROUNDS = (1, 2, 3, 4)


def propagated(k, s):
    return -2 * k + 1 + s, 2 * k - s


def new_blocks(call, s):
    low, high = propagated(ROUNDS[call], s)
    if call:
        low_before, high_before = propagated(ROUNDS[call - 1], s)
        if ROUNDS[call] == ZS // 2:
            return [(high_before + 1, BLOCKS + low_before - 1)]
        if low_before <= high_before:
            return [(low, low_before - 1), (high_before + 1, high)]
    return [(low, high)] if low <= high else []


def kept_blocks(call, s):
    k = ROUNDS[call]
    low, high = -2 * k + s, 2 * k + 1 - s
    return (low, low + 1, high - 1, high) if low <= high else ()


def members(runs):
    return [e for low, high in runs for e in range(low, high + 1)]


def slots_of(call, s):
    return {e: at + 1 for at, e in enumerate(members([(low - 1, high + 1) for low, high in new_blocks(call, s)]))}


def handed_on(call, s):
    kept = {e % BLOCKS: at for at, e in enumerate(kept_blocks(call - 1, s))} if call else {}
    return {e: (slot, kept[e % BLOCKS]) for e, slot in slots_of(call, s).items() if e % BLOCKS in kept}


def fresh_of(call):
    return {e: slot for e, slot in slots_of(call, 0).items() if e not in handed_on(call, 0)}


def trans_of(call, s):
    return {e: at for at, e in enumerate(members(new_blocks(call, s - 1)))}


def zs_of(call):
    wanted = set(fresh_of(call))
    for s in range(1, SLICES):
        wanted |= set(trans_of(call, s))
    return {(e // 2) % ZS for e in wanted}


def body(call, holders, where_ref, *refs):
    refs = list(refs)

    def take(n):
        taken = refs[:n]
        del refs[:n]
        return taken

    last = call == len(ROUNDS) - 1
    pieces = take(len(holders))
    (weights,), rows_band, (x_wave, y_wave) = take(1), take(SLICES), take(2)
    kept_in = take(SLICES) if call else None
    earlier_calls = [c for c in range(call) if new_blocks(c, SLICES - 1)] if last else []
    done = take(len(earlier_calls))
    (out,) = take(1) if last else (None,)
    kept_out = None if last else take(SLICES)
    made = refs.pop(0) if not last and new_blocks(call, SLICES - 1) else None
    trans, fields = take(SLICES - 1), take(SLICES)
    if last:
        made, sems = take(2)
    z0, core, lo, rank = where_ref[0], where_ref[1], where_ref[2], where_ref[3]
    sign = 1 - 2 * core
    slots = [slots_of(call, s) for s in range(SLICES)]

    def half_of(e):
        return core if e % 2 == 0 else 1 - core

    def plane_block(e):
        return 2 * lax.rem(z0 + sign * (e // 2) + 2 * ZS, ZS) + half_of(e)

    def parts_of(e):
        index = jnp.where(half_of(e) == lo, 0, 1)
        sides = set()
        for ref, entries in zip(pieces, holders):
            for number, (z_at, mine) in enumerate(entries):
                if (z_at - e // 2) % ZS == 0 and mine not in sides:
                    sides.add(mine)
                    yield ref, 2 * number + index, core if mine else 1 - core

    copies = []

    def write(block, e):
        columns = pl.ds(pl.multiple_of(plane_block(e) * LANES, LANES), LANES)
        copies.append(pltpu.make_async_copy(block, out.at[:, :, :, columns], sems.at[len(copies)]))
        copies[-1].start()

    for earlier, blocks in zip(earlier_calls, done):
        for number, e in enumerate(members(new_blocks(earlier, SLICES - 1))):
            write(blocks.at[number], e)

    for s in range(SLICES):
        fields[s][0] = jnp.zeros(fields[s].shape[1:], fields[s].dtype)
        for slot, at in handed_on(call, s).values():
            fields[s][slot] = kept_in[s][at]

    for e, at in fresh_of(call).items():
        kept = [] if last else [kept_out[0].at[k] for k, kept_e in enumerate(kept_blocks(call, 0)) if kept_e == e]
        b = plane_block(e)
        for ref, index, side in parts_of(e):
            t_re, t_im = cosine_sine(ref[index, 0 : HALF[0], :].astype(jnp.float32))
            for wv in range(2):
                rows = pl.ds(pl.multiple_of(side * HALF[0], 16), HALF[0])
                x_re, x_im = x_wave[b, wv, 0:1, :], x_wave[b, wv, 1:2, :]
                y_re, y_im = y_wave[wv, 0, rows, :], y_wave[wv, 1, rows, :]
                re, im = x_re * y_re - x_im * y_im, x_re * y_im + x_im * y_re
                rows = pl.ds(pl.multiple_of(wv * IN_ROWS[0] + side * HALF[0], 16), HALF[0])
                for target in (fields[0].at[at], *kept):
                    target[rows, 0:LANES] = (re * t_re - im * t_im).astype(jnp.bfloat16)
                    target[rows, LANES:] = (re * t_im + im * t_re).astype(jnp.bfloat16)
    for s in range(1, SLICES):
        for e, at in trans_of(call, s).items():
            for ref, index, side in parts_of(e):
                re, im = cosine_sine(ref[index, HALF_AT[s] : HALF_AT[s] + HALF[s], :].astype(jnp.float32))
                rows = pl.ds(pl.multiple_of(side * HALF[s], 16), HALF[s])
                trans[s - 1][at, rows, 0:LANES] = re.astype(jnp.bfloat16)
                trans[s - 1][at, rows, LANES:] = im.astype(jnp.bfloat16)

    for s in range(SLICES):
        rows_in, rows_out = IN_ROWS[s], IN_ROWS[s] - 2 * REACH
        lane = lax.broadcasted_iota(jnp.int32, (2 * rows_in, 2 * LANES), 1)
        from_left = (lane & (LANES - 1)) >= LANES // 2
        blocks = members(new_blocks(call, s))
        halves = []
        for e in blocks:
            at, b = slots[s][e], plane_block(e)
            left = fields[s][jnp.where(b == 0, 0, at - sign)]
            right = fields[s][jnp.where(b == BLOCKS - 1, 0, at + sign)]
            both = jnp.concatenate([fields[s][at], jnp.where(from_left, left, right)], axis=1)
            h = jnp.dot(both, weights[...], preferred_element_type=jnp.float32).astype(jnp.bfloat16)
            re = jnp.concatenate([h[:rows_in, :LANES], h[rows_in:, :LANES]], axis=1)
            im = jnp.concatenate([h[:rows_in, LANES:], h[rows_in:, LANES:]], axis=1)
            halves.append(jnp.concatenate([re, im], axis=0))
        for number, (e, h) in enumerate(zip(blocks, halves)):
            full = jnp.dot(rows_band[s][...], h, preferred_element_type=jnp.float32)
            for wv in range(2):
                re = full[:rows_out, wv * LANES : (wv + 1) * LANES]
                im = full[rows_out:, wv * LANES : (wv + 1) * LANES]
                if s + 1 < SLICES:
                    t = trans[s].at[trans_of(call, s + 1)[e]]
                    t_re, t_im = t[:, :LANES].astype(jnp.float32), t[:, LANES:].astype(jnp.float32)
                    re, im = (re * t_re - im * t_im).astype(jnp.bfloat16), (re * t_im + im * t_re).astype(jnp.bfloat16)
                    rows = slice(wv * rows_out, (wv + 1) * rows_out)
                    targets = [fields[s + 1].at[slots[s + 1][e]]] if e in slots[s + 1] else []
                    if not last:
                        kept = kept_blocks(call, s + 1)
                        targets += [kept_out[s + 1].at[at] for at, kept_e in enumerate(kept) if kept_e == e]
                    for target in targets:
                        target[rows, 0:LANES] = re
                        target[rows, LANES:] = im
                else:
                    made[number, 0, wv] = re.astype(jnp.bfloat16)
                    made[number, 1, wv] = im.astype(jnp.bfloat16)
            if last and s + 1 == SLICES:
                write(made.at[number], e)

    for copy in copies:
        copy.wait()


def propagate(call, holders, where, pieces, constants, kept, done):
    last = call == len(ROUNDS) - 1
    vmem, anywhere = pl.BlockSpec(memory_space=pltpu.VMEM), pl.BlockSpec(memory_space=pl.ANY)
    operands = [*pieces, *constants, *kept, *(done if last else ())]
    made = len(members(new_blocks(call, SLICES - 1)))
    scratch = [pltpu.VMEM((max(1, len(trans_of(call, s))), IN_ROWS[s], 2 * LANES), jnp.bfloat16) for s in range(1, SLICES)]
    scratch += [pltpu.VMEM((len(slots_of(call, s)) + 1, 2 * IN_ROWS[s], 2 * LANES), jnp.bfloat16) for s in range(SLICES)]
    if last:
        shapes = [jax.ShapeDtypeStruct((2, 2, ROWS, NX), jnp.bfloat16)]
        scratch += [pltpu.VMEM((made, 2, 2, ROWS, LANES), jnp.bfloat16), pltpu.SemaphoreType.DMA((BLOCKS,))]
    else:
        shapes = [jax.ShapeDtypeStruct((4, 2 * n, 2 * LANES), jnp.bfloat16) for n in IN_ROWS]
        if made:
            shapes += [jax.ShapeDtypeStruct((made, 2, 2, ROWS, LANES), jnp.bfloat16)]
    return pl.pallas_call(
        functools.partial(body, call, holders),
        out_shape=shapes,
        in_specs=[pl.BlockSpec(memory_space=pltpu.SMEM)] + [vmem] * len(operands),
        out_specs=[anywhere if last else vmem] * len(shapes),
        scratch_shapes=scratch,
        compiler_params=pltpu.CompilerParams(vmem_limit_bytes=40 * 2**20),
        cost_estimate=pl.CostEstimate(flops=(7 if call else 4) * 10**9, bytes_accessed=2**20, transcendentals=0),
    )(where, *operands)


def per_device(potential, tilt_index):
    wave_at, rank = lax.axis_index("wave"), lax.axis_index("rows")
    z, lo, core = wave_at // 4, (wave_at // 2) % 2, wave_at % 2
    first = core == 0

    def by_core(mine, other):
        return jnp.concatenate([jnp.where(first, mine, other), jnp.where(first, other, mine)], axis=-1)

    pair = send(potential, to_pair)
    own = by_core(potential, send(potential, to_core))
    pair = by_core(pair, send(pair, to_core))
    rows = jnp.stack([own, pair])
    down = [rows[:, s, ROWS - HALO[s] :] for s in range(SLICES)]
    up = [rows[:, s, : HALO[s]] for s in range(SLICES)]
    halo = send(jnp.where(first, jnp.concatenate(down, axis=1), jnp.concatenate(up, axis=1)), to_rank)

    top, bottom = [], []
    for s in range(SLICES):
        piece = halo[:, sum(HALO[:s]) : sum(HALO[: s + 1])]
        top += [piece, rows[:, s, :CORE_ROWS]]
        bottom += [rows[:, s, CORE_ROWS:], piece]
    mine = jnp.where(first, jnp.concatenate(top, axis=1), jnp.concatenate(bottom, axis=1))
    other = send(mine, to_core)

    tilt_index, _ = lax.optimization_barrier((tilt_index, halo))
    y = rank * ROWS - HALO[0] + jnp.arange(IN_ROWS[0], dtype=jnp.int32)
    inside = ((y >= 0) & (y < NY)).astype(jnp.float32)
    turn_y = (tilt_index[:, 0:1] * y[None, :] % NY).astype(jnp.float32) * (2.0 * math.pi / NY)
    y_wave = jnp.stack([jnp.cos(turn_y) * inside, jnp.sin(turn_y) * inside], axis=1)
    y_wave = jnp.broadcast_to(y_wave[..., None], (*y_wave.shape, LANES))
    x = jnp.arange(NX, dtype=jnp.int32)
    turn_x = (tilt_index[:, 1:2] * x[None, :] % NX).astype(jnp.float32) * (2.0 * math.pi / NX)
    x_wave = jnp.stack([jnp.cos(turn_x), jnp.sin(turn_x)], axis=1)
    x_wave = x_wave.reshape(2, 2, BLOCKS, LANES).transpose(2, 0, 1, 3)
    constants = [jnp.asarray(column_weights(), jnp.bfloat16)]
    for s in range(SLICES):
        y = rank * ROWS - HALO[s] + REACH + jnp.arange(IN_ROWS[s] - 2 * REACH, dtype=jnp.int32)
        keep = jnp.tile((y >= 0) & (y < NY), 2)[:, None]
        constants.append(jnp.where(keep, jnp.asarray(row_weights(s), jnp.bfloat16), 0))
    constants += [x_wave, y_wave]
    where = jnp.stack([z, core, lo, rank]).astype(jnp.int32)

    held = {((0, True),): mine, ((0, False),): other}
    calls = []
    for k in range(1, ZS // 2 + 1):
        mine, other = send(mine, to_next), send(other, to_next)
        if calls and k < ZS // 2:
            mine, other, _ = lax.optimization_barrier((mine, other, calls[-1][0]))
        held[((-k, True),)], held[((-k, False),)] = mine, other
        if k < ZS // 2:
            held[(k, False), (k, True)] = send(jnp.concatenate([mine, other], axis=0), to_core)
        if k in ROUNDS:
            call = ROUNDS.index(k)
            holders = tuple(key for key in held if key[0][0] % ZS in zs_of(call))
            pieces = [held[key] for key in holders]
            if k == ZS // 2:
                pieces[-1], _ = lax.optimization_barrier((pieces[-1], calls[-1][0]))
            kept = calls[-1][:SLICES] if calls else []
            done = [made[SLICES] for made in calls if len(made) > SLICES]
            calls.append(propagate(call, holders, where, pieces, constants, kept, done))
    return calls[-1][0]


def solution(mesh):
    return jax.shard_map(
        per_device,
        mesh=mesh,
        in_specs=(P(None, "rows", "wave"), P("wave", None)),
        out_specs=P(None, "wave", "rows", None),
        check_vma=False,
    )
```

profile of v0, /device:TPU:16, one launch (start us, length us, event | category | flops | bytes accessed | tf_op | source)
XLA Modules:
  0.0 58.2 jit_solution(12781116939621081229)
XLA Ops:
  0.0 1.5 %collective-permute-start.1 = (bf16[4,64,64]{2,1,0:T(8,128)(2,1)}, bf16[4,64,64]{2,1,0:T(8,128)(2,1)S(1)}, u32[]{:S(2)}, u32[]{:S(2)}) collective-permute-start(bf16[4,64,64]{2,1,0:T(8,128)(2,1)} %param.7), channel_id=1, source_target_pairs={{0,16},{1,17},{2,18},{3,19},{4,20},{5,21},{6,22},{7,23},{8,24},{9,... | collective-permute-start | bytes 98312 | tf_op jit(solution)/shard_map/ppermute | solution.py:44
  1.5 0.0 collective-permute-start
  1.6 0.1 broadcast_in_dim.66
  1.7 0.1 broadcast_in_dim.72
  1.8 0.1 broadcast_in_dim.75
  1.9 0.0 copy-start.1
  1.9 1.1 %broadcast_select_fusion.refs_6_.refs_9_.refs_10_ = bf16[320,384]{1,0:T(8,128)(2,1)S(1)} fusion(bf16[320,384]{1,0:T(8,128)(2,1)} %constant.123.clone, pred[320]{0:T(512)(128)(4,1)S(1)} %broadcast_in_dim.66), kind=kLoop, calls=%fused_computation.27 | loop fusion | flops 122880 | bytes 491840 | tf_op jit(solution)/shard_map/jit(_where)/select_n | solution.py:352
  3.0 0.0 copy-done.1
  3.0 0.0 copy-start.2
  3.1 0.1 broadcast_select_fusion.1.refs_7_.refs_10_.refs_11_
  3.2 0.8 %copy-done.2 = bf16[192,256]{1,0:T(8,128)(2,1)S(1)} copy-done((bf16[192,256]{1,0:T(8,128)(2,1)S(1)}, bf16[192,256]{1,0:T(8,128)(2,1)}, u32[]{:S(2)}) %copy-start.2) | copy-done | bytes 98328
  3.9 0.0 copy-start.3
  3.9 0.1 broadcast_select_fusion.3.refs_8_.refs_11_.refs_12_
  4.0 0.7 %copy-done.3 = bf16[128,192]{1,0:T(8,128)(2,1)S(1)} copy-done((bf16[128,192]{1,0:T(8,128)(2,1)S(1)}, bf16[128,192]{1,0:T(8,128)(2,1)}, u32[]{:S(2)}) %copy-start.3) | copy-done | bytes 49176
  4.8 0.0 copy-start.4
  4.8 0.1 broadcast_select_fusion.4.refs_9_.refs_12_.refs_13_
  4.9 0.1 pad_add_fusion.where_ref
  4.9 0.0 collective-permute-done.1
  5.0 0.5 collective-permute-start.2
  5.5 0.0 collective-permute-done
  5.5 0.1 copy-done.4
  5.6 0.8 %collective-permute-done.2 = bf16[4,64,64]{2,1,0:T(8,128)(2,1)S(1)} collective-permute-done((bf16[4,64,64]{2,1,0:T(8,128)(2,1)S(1)}, bf16[4,64,64]{2,1,0:T(8,128)(2,1)S(1)}, u32[]{:S(2)}, u32[]{:S(2)}) %collective-permute-start.2) | collective-permute-done | bytes 32800 | tf_op jit(solution)/shard_map/ppermute | solution.py:44
  6.4 0.1 maximum_bitcast_fusion
  6.6 4.6 %collective-permute-start.3 = (bf16[2,160,128]{2,1,0:T(8,128)(2,1)S(1)}, bf16[2,160,128]{2,1,0:T(8,128)(2,1)S(1)}, u32[]{:S(2)}, u32[]{:S(2)}) collective-permute-start(bf16[2,160,128]{2,1,0:T(8,128)(2,1)S(1)} %fusion.2), channel_id=1, source_target_pairs={{0,1},{1,2},{2,3},{3,4},{4,5},{5,6},{6,7},{9,8},{10,9},{11,10},{12... | collective-permute-start | bytes 245768 | tf_op jit(solution)/shard_map/ppermute | solution.py:44
  11.3 4.1 %collective-permute-done.3 = bf16[2,160,128]{2,1,0:T(8,128)(2,1)S(1)} collective-permute-done((bf16[2,160,128]{2,1,0:T(8,128)(2,1)S(1)}, bf16[2,160,128]{2,1,0:T(8,128)(2,1)S(1)}, u32[]{:S(2)}, u32[]{:S(2)}) %collective-permute-start.3) | collective-permute-done | bytes 81952 | tf_op jit(solution)/shard_map/ppermute | solution.py:44
  15.5 0.0 copy-start.5
  15.6 0.1 collective-permute-start.6
  15.7 2.0 %collective-permute-start.4 = (bf16[2,288,128]{2,1,0:T(8,128)(2,1)S(1)}, bf16[2,288,128]{2,1,0:T(8,128)(2,1)S(1)}, u32[]{:S(2)}, u32[]{:S(2)}) collective-permute-start(bf16[2,288,128]{2,1,0:T(8,128)(2,1)S(1)} %broadcast_select_fusion.2.refs_0_), channel_id=1, source_target_pairs={{0,32},{1,33},{2,34},{3,35},{4,36},{5,37},{6,38},{7,39},{8,232},{9... | collective-permute-start | bytes 442376 | tf_op jit(solution)/shard_map/ppermute | solution.py:44
  17.6 0.0 copy-done.5
  17.7 0.2 slice_reduce_fusion
  17.8 0.1 fusion.18
  17.9 0.0 collective-permute-done.6.refs_1_
  17.9 2.0 %collective-permute-start.7 = (bf16[2,288,128]{2,1,0:T(8,128)(2,1)S(1)}, bf16[2,288,128]{2,1,0:T(8,128)(2,1)S(1)}, u32[]{:S(2)}, u32[]{:S(2)}) collective-permute-start(bf16[2,288,128]{2,1,0:T(8,128)(2,1)S(1)} %collective-permute-done.6.refs_1_), channel_id=1, source_target_pairs={{0,32},{1,33},{2,34},{3,35},{4,36},{5,37},{6,38},{7,39},{8,232},{9... | collective-permute-start | bytes 442376 | tf_op jit(solution)/shard_map/ppermute | solution.py:44
  19.9 0.2 cosine_multiply_fusion
  20.1 4.6 %collective-permute-done.4.refs_2_.refs_0_ = bf16[2,288,128]{2,1,0:T(8,128)(2,1)S(1)} collective-permute-done((bf16[2,288,128]{2,1,0:T(8,128)(2,1)S(1)}, bf16[2,288,128]{2,1,0:T(8,128)(2,1)S(1)}, u32[]{:S(2)}, u32[]{:S(2)}) %collective-permute-start.4) | collective-permute-done | bytes 147488 | tf_op jit(solution)/shard_map/ppermute | solution.py:44
  24.7 1.6 %collective-permute-done.7.refs_3_.refs_1_ = bf16[2,288,128]{2,1,0:T(8,128)(2,1)S(1)} collective-permute-done((bf16[2,288,128]{2,1,0:T(8,128)(2,1)S(1)}, bf16[2,288,128]{2,1,0:T(8,128)(2,1)S(1)}, u32[]{:S(2)}, u32[]{:S(2)}) %collective-permute-start.7) | collective-permute-done | bytes 147488 | tf_op jit(solution)/shard_map/ppermute | solution.py:44
  26.3 0.0 copy-start
  26.3 0.2 collective-permute-start.9
  26.5 0.5 fusion.31
  27.0 0.1 collective-permute-start.5
  27.1 1.3 %collective-permute-start.8 = (bf16[2,288,128]{2,1,0:T(8,128)(2,1)S(1)}, bf16[2,288,128]{2,1,0:T(8,128)(2,1)S(1)}, u32[]{:S(2)}, u32[]{:S(2)}) collective-permute-start(bf16[2,288,128]{2,1,0:T(8,128)(2,1)S(1)} %collective-permute-done.7.refs_3_.refs_1_), channel_id=1, source_target_pairs={{0,32},{1,33},{2,34},{3,35},{4,36},{5,37},{6,38},{7,39},{8,232},{9... | collective-permute-start | bytes 442376 | tf_op jit(solution)/shard_map/ppermute | solution.py:44
  28.4 0.0 collective-permute-done.9.refs_4_.refs_2_
  28.4 0.2 broadcast_in_dim.78.refs_11_.refs_14_.refs_15_
  28.6 0.0 copy-done
  28.6 3.5 %shard_map.73 = (bf16[4,384,256]{2,1,0:T(8,128)(2,1)S(1)}, bf16[4,320,256]{2,1,0:T(8,128)(2,1)S(1)}, bf16[4,256,256]{2,1,0:T(8,128)(2,1)S(1)}, bf16[4,192,256]{2,1,0:T(8,128)(2,1)S(1)}) custom-call(s32[4]{0:T(128)S(1)} %pad_add_fusion.where_ref, bf16[2,288,128]{2,1,0:T(8,128)(2,1)S(1)} %broadcast_select_fusion.2.refs_0_, ...), custom_call_target="tpu_custom_call" | custom-call | flops 4000000000 | bytes 1048576 | tf_op jit(solution)/shard_map/pallas_call | solution.py:303
  32.1 1.3 %collective-permute-done.5.refs_5_.refs_3_.refs_0_ = bf16[2,288,128]{2,1,0:T(8,128)(2,1)S(1)} collective-permute-done((bf16[2,288,128]{2,1,0:T(8,128)(2,1)S(1)}, bf16[2,288,128]{2,1,0:T(8,128)(2,1)S(1)}, u32[]{:S(2)}, u32[]{:S(2)}) %collective-permute-start.5) | collective-permute-done | bytes 147488 | tf_op jit(solution)/shard_map/ppermute | solution.py:44
  33.5 1.6 %collective-permute-done.8.refs_6_.refs_4_.refs_1_ = bf16[2,288,128]{2,1,0:T(8,128)(2,1)S(1)} collective-permute-done((bf16[2,288,128]{2,1,0:T(8,128)(2,1)S(1)}, bf16[2,288,128]{2,1,0:T(8,128)(2,1)S(1)}, u32[]{:S(2)}, u32[]{:S(2)}) %collective-permute-start.8) | collective-permute-done | bytes 147488 | tf_op jit(solution)/shard_map/ppermute | solution.py:44
  35.1 0.1 collective-permute-start.10
  35.2 0.1 collective-permute-start.11
  35.3 2.0 %collective-permute-start.12 = (bf16[2,288,128]{2,1,0:T(8,128)(2,1)S(1)}, bf16[2,288,128]{2,1,0:T(8,128)(2,1)S(1)}, u32[]{:S(2)}, u32[]{:S(2)}) collective-permute-start(bf16[2,288,128]{2,1,0:T(8,128)(2,1)S(1)} %collective-permute-done.8.refs_6_.refs_4_.refs_1_), channel_id=1, source_target_pairs={{0,32},{1,33},{2,34},{3,35},{4,36},{5,37},{6,38},{7,39},{8,232},{9... | collective-permute-start | bytes 442376 | tf_op jit(solution)/shard_map/ppermute | solution.py:44
  37.2 0.0 collective-permute-done.10.refs_7_.refs_5_.refs_2_
  37.2 4.8 %shard_map.74 = (bf16[4,384,256]{2,1,0:T(8,128)(2,1)S(1)}, bf16[4,320,256]{2,1,0:T(8,128)(2,1)S(1)}, bf16[4,256,256]{2,1,0:T(8,128)(2,1)S(1)}, bf16[4,192,256]{2...) custom-call(s32[4]{0:T(128)S(1)} %pad_add_fusion.where_ref, bf16[2,288,128]{2,1,0:T(8,128)(2,1)S(1)} %broadcast_select_fusion.2.refs_0_, ...), custom_call_target="tpu_custom_call" | custom-call | flops 7000000000 | bytes 1048576 | tf_op jit(solution)/shard_map/pallas_call | solution.py:303
  42.0 0.0 collective-permute-done.11.refs_6_.refs_3_
  42.0 1.1 %collective-permute-done.12.refs_7_.refs_4_ = bf16[2,288,128]{2,1,0:T(8,128)(2,1)S(1)} collective-permute-done((bf16[2,288,128]{2,1,0:T(8,128)(2,1)S(1)}, bf16[2,288,128]{2,1,0:T(8,128)(2,1)S(1)}, u32[]{:S(2)}, u32[]{:S(2)}) %collective-permute-start.12) | collective-permute-done | bytes 147488 | tf_op jit(solution)/shard_map/ppermute | solution.py:44
  43.2 0.1 collective-permute-start.13
  43.3 0.4 collective-permute-start.15
  43.7 2.8 %collective-permute-start.14 = (bf16[2,288,128]{2,1,0:T(8,128)(2,1)S(1)}, bf16[2,288,128]{2,1,0:T(8,128)(2,1)S(1)}, u32[]{:S(2)}, u32[]{:S(2)}) collective-permute-start(bf16[2,288,128]{2,1,0:T(8,128)(2,1)S(1)} %collective-permute-done.11.refs_6_.refs_3_), channel_id=1, source_target_pairs={{0,32},{1,33},{2,34},{3,35},{4,36},{5,37},{6,38},{7,39},{8,232},{9... | collective-permute-start | bytes 442376 | tf_op jit(solution)/shard_map/ppermute | solution.py:44
  46.4 0.0 collective-permute-done.13.refs_8_.refs_5_
  46.5 4.9 %shard_map.75 = (bf16[4,384,256]{2,1,0:T(8,128)(2,1)S(1)}, bf16[4,320,256]{2,1,0:T(8,128)(2,1)S(1)}, bf16[4,256,256]{2,1,0:T(8,128)(2,1)S(1)}, bf16[4,192,256]{2...) custom-call(s32[4]{0:T(128)S(1)} %pad_add_fusion.where_ref, ...), custom_call_target="tpu_custom_call" | custom-call | flops 7000000000 | bytes 1048576 | tf_op jit(solution)/shard_map/pallas_call | solution.py:303
  51.4 0.0 collective-permute-done.15.refs_7_
  51.4 0.0 collective-permute-done.14.refs_6_
  51.4 6.7 %shard_map.76 = bf16[2,2,64,2048]{3,2,1,0:T(8,128)(2,1)} custom-call(s32[4]{0:T(128)S(1)} %pad_add_fusion.where_ref, bf16[2,288,128]{2,1,0:T(8,128)(2,1)S(1)} %collective-permute-done.5.refs_5_.refs_3_.refs_0_, bf16[2,288,128]{2,1,0:T(8,128)(2,1)S(1)} %collective-permute-done.8.refs_6_.refs_4_.refs_1_, ...), custom_call_target="tpu_custom_call" | custom-call | flops 7000000000 | bytes 1048576 | tf_op jit(solution)/shard_map/pallas_call | solution.py:303
  (37 shorter events, 0.4 us)
Async XLA Ops:
  0.0 5.0 %collective-permute-start.1 = (bf16[4,64,64]{2,1,0:T(8,128)(2,1)}, bf16[4,64,64]{2,1,0:T(8,128)(2,1)S(1)}, u32[]{:S(2)}, u32[]{:S(2)}) collective-permute-start(bf16[4,64,64]{2,1,0:T(8,128)(2,1)} %param.7), channel_id=1, source_target_pairs={{0,16},{1,17},{2,18},{3,19},{4,20},{5,21},{6,22},{7,23},{8,24},{9,... | collective-permute-start | bytes 98312 | tf_op jit(solution)/shard_map/ppermute | solution.py:44
  1.5 4.0 %collective-permute-start = (bf16[4,64,64]{2,1,0:T(8,128)(2,1)}, bf16[4,64,64]{2,1,0:T(8,128)(2,1)S(1)}, u32[]{:S(2)}, u32[]{:S(2)}) collective-permute-start(bf16[4,64,64]{2,1,0:T(8,128)(2,1)} %param.7), channel_id=1, source_target_pairs={{0,8},{1,9},{2,10},{3,11},{4,12},{5,13},{6,14},{7,15},{8,0},{9,1},... | collective-permute-start | bytes 98312 | tf_op jit(solution)/shard_map/ppermute | solution.py:44
  1.9 1.1 %copy-start.1 = (bf16[256,320]{1,0:T(8,128)(2,1)S(1)}, bf16[256,320]{1,0:T(8,128)(2,1)}, u32[]{:S(2)}) copy-start(bf16[256,320]{1,0:T(8,128)(2,1)} %constant.124.clone) | copy-start | bytes 491524
  3.0 0.9 %copy-start.2 = (bf16[192,256]{1,0:T(8,128)(2,1)S(1)}, bf16[192,256]{1,0:T(8,128)(2,1)}, u32[]{:S(2)}) copy-start(bf16[192,256]{1,0:T(8,128)(2,1)} %constant.125.clone) | copy-start | bytes 294916
  3.9 0.8 %copy-start.3 = (bf16[128,192]{1,0:T(8,128)(2,1)S(1)}, bf16[128,192]{1,0:T(8,128)(2,1)}, u32[]{:S(2)}) copy-start(bf16[128,192]{1,0:T(8,128)(2,1)} %constant.126.clone) | copy-start | bytes 147460
  4.8 0.8 %copy-start.4 = (bf16[4,64,64]{2,1,0:T(8,128)(2,1)S(1)}, bf16[4,64,64]{2,1,0:T(8,128)(2,1)}, u32[]{:S(2)}) copy-start(bf16[4,64,64]{2,1,0:T(8,128)(2,1)} %param.7) | copy-start | bytes 98308
  5.0 1.4 %collective-permute-start.2 = (bf16[4,64,64]{2,1,0:T(8,128)(2,1)S(1)}, bf16[4,64,64]{2,1,0:T(8,128)(2,1)S(1)}, u32[]{:S(2)}, u32[]{:S(2)}) collective-permute-start(bf16[4,64,64]{2,1,0:T(8,128)(2,1)S(1)} %collective-permute-done.1), channel_id=1, source_target_pairs={{0,8},{1,9},{2,10},{3,11},{4,12},{5,13},{6,14},{7,15},{8,0},{9,1},... | collective-permute-start | bytes 98312 | tf_op jit(solution)/shard_map/ppermute | solution.py:44
  6.6 8.7 %collective-permute-start.3 = (bf16[2,160,128]{2,1,0:T(8,128)(2,1)S(1)}, bf16[2,160,128]{2,1,0:T(8,128)(2,1)S(1)}, u32[]{:S(2)}, u32[]{:S(2)}) collective-permute-start(bf16[2,160,128]{2,1,0:T(8,128)(2,1)S(1)} %fusion.2), channel_id=1, source_target_pairs={{0,1},{1,2},{2,3},{3,4},{4,5},{5,6},{6,7},{9,8},{10,9},{11,10},{12... | collective-permute-start | bytes 245768 | tf_op jit(solution)/shard_map/ppermute | solution.py:44
  15.5 2.1 %copy-start.5 = (s32[2,2]{1,0:T(2,128)S(1)}, s32[2,2]{1,0:T(2,128)}, u32[]{:S(2)}) copy-start(s32[2,2]{1,0:T(2,128)} %param.8) | copy-start | bytes 52
  15.6 2.4 %collective-permute-start.6 = (bf16[2,288,128]{2,1,0:T(8,128)(2,1)S(1)}, bf16[2,288,128]{2,1,0:T(8,128)(2,1)S(1)}, u32[]{:S(2)}, u32[]{:S(2)}) collective-permute-start(bf16[2,288,128]{2,1,0:T(8,128)(2,1)S(1)} %broadcast_select_fusion.2.refs_0_), channel_id=1, source_target_pairs={{0,8},{1,9},{2,10},{3,11},{4,12},{5,13},{6,14},{7,15},{8,0},{9,1},... | collective-permute-start | bytes 442376 | tf_op jit(solution)/shard_map/ppermute | solution.py:44
  15.7 9.1 %collective-permute-start.4 = (bf16[2,288,128]{2,1,0:T(8,128)(2,1)S(1)}, bf16[2,288,128]{2,1,0:T(8,128)(2,1)S(1)}, u32[]{:S(2)}, u32[]{:S(2)}) collective-permute-start(bf16[2,288,128]{2,1,0:T(8,128)(2,1)S(1)} %broadcast_select_fusion.2.refs_0_), channel_id=1, source_target_pairs={{0,32},{1,33},{2,34},{3,35},{4,36},{5,37},{6,38},{7,39},{8,232},{9... | collective-permute-start | bytes 442376 | tf_op jit(solution)/shard_map/ppermute | solution.py:44
  17.9 8.4 %collective-permute-start.7 = (bf16[2,288,128]{2,1,0:T(8,128)(2,1)S(1)}, bf16[2,288,128]{2,1,0:T(8,128)(2,1)S(1)}, u32[]{:S(2)}, u32[]{:S(2)}) collective-permute-start(bf16[2,288,128]{2,1,0:T(8,128)(2,1)S(1)} %collective-permute-done.6.refs_1_), channel_id=1, source_target_pairs={{0,32},{1,33},{2,34},{3,35},{4,36},{5,37},{6,38},{7,39},{8,232},{9... | collective-permute-start | bytes 442376 | tf_op jit(solution)/shard_map/ppermute | solution.py:44
  26.3 2.2 %copy-start = (bf16[512,256]{1,0:T(8,128)(2,1)S(1)}, bf16[512,256]{1,0:T(8,128)(2,1)}, u32[]{:S(2)}) copy-start(bf16[512,256]{1,0:T(8,128)(2,1)} %constant.122.clone.refs_5_.refs_8_.refs_9_) | copy-start | bytes 786436
  26.3 2.1 %collective-permute-start.9 = (bf16[4,288,128]{2,1,0:T(8,128)(2,1)S(1)}, bf16[4,288,128]{2,1,0:T(8,128)(2,1)S(1)}, u32[]{:S(2)}, u32[]{:S(2)}) collective-permute-start(bf16[4,288,128]{2,1,0:T(8,128)(2,1)S(1)} %pad_maximum_fusion), channel_id=1, source_target_pairs={{0,8},{1,9},{2,10},{3,11},{4,12},{5,13},{6,14},{7,15},{8,0},{9,1},... | collective-permute-start | bytes 884744 | tf_op jit(solution)/shard_map/ppermute | solution.py:44
  27.0 6.4 %collective-permute-start.5 = (bf16[2,288,128]{2,1,0:T(8,128)(2,1)S(1)}, bf16[2,288,128]{2,1,0:T(8,128)(2,1)S(1)}, u32[]{:S(2)}, u32[]{:S(2)}) collective-permute-start(bf16[2,288,128]{2,1,0:T(8,128)(2,1)S(1)} %collective-permute-done.4.refs_2_.refs_0_), channel_id=1, source_target_pairs={{0,32},{1,33},{2,34},{3,35},{4,36},{5,37},{6,38},{7,39},{8,232},{9... | collective-permute-start | bytes 442376 | tf_op jit(solution)/shard_map/ppermute | solution.py:44
  27.1 7.9 %collective-permute-start.8 = (bf16[2,288,128]{2,1,0:T(8,128)(2,1)S(1)}, bf16[2,288,128]{2,1,0:T(8,128)(2,1)S(1)}, u32[]{:S(2)}, u32[]{:S(2)}) collective-permute-start(bf16[2,288,128]{2,1,0:T(8,128)(2,1)S(1)} %collective-permute-done.7.refs_3_.refs_1_), channel_id=1, source_target_pairs={{0,32},{1,33},{2,34},{3,35},{4,36},{5,37},{6,38},{7,39},{8,232},{9... | collective-permute-start | bytes 442376 | tf_op jit(solution)/shard_map/ppermute | solution.py:44
  35.1 2.2 %collective-permute-start.10 = (bf16[4,288,128]{2,1,0:T(8,128)(2,1)S(1)}, bf16[4,288,128]{2,1,0:T(8,128)(2,1)S(1)}, u32[]{:S(2)}, u32[]{:S(2)}) collective-permute-start(bf16[4,288,128]{2,1,0:T(8,128)(2,1)S(1)} %pad_maximum_fusion.1), channel_id=1, source_target_pairs={{0,8},{1,9},{2,10},{3,11},{4,12},{5,13},{6,14},{7,15},{8,0},{9,1},... | collective-permute-start | bytes 884744 | tf_op jit(solution)/shard_map/ppermute | solution.py:44
  35.2 6.9 %collective-permute-start.11 = (bf16[2,288,128]{2,1,0:T(8,128)(2,1)S(1)}, bf16[2,288,128]{2,1,0:T(8,128)(2,1)S(1)}, u32[]{:S(2)}, u32[]{:S(2)}) collective-permute-start(bf16[2,288,128]{2,1,0:T(8,128)(2,1)S(1)} %collective-permute-done.5.refs_5_.refs_3_.refs_0_), channel_id=1, source_target_pairs={{0,32},{1,33},{2,34},{3,35},{4,36},{5,37},{6,38},{7,39},{8,232},{9... | collective-permute-start | bytes 442376 | tf_op jit(solution)/shard_map/ppermute | solution.py:44
  35.3 7.9 %collective-permute-start.12 = (bf16[2,288,128]{2,1,0:T(8,128)(2,1)S(1)}, bf16[2,288,128]{2,1,0:T(8,128)(2,1)S(1)}, u32[]{:S(2)}, u32[]{:S(2)}) collective-permute-start(bf16[2,288,128]{2,1,0:T(8,128)(2,1)S(1)} %collective-permute-done.8.refs_6_.refs_4_.refs_1_), channel_id=1, source_target_pairs={{0,32},{1,33},{2,34},{3,35},{4,36},{5,37},{6,38},{7,39},{8,232},{9... | collective-permute-start | bytes 442376 | tf_op jit(solution)/shard_map/ppermute | solution.py:44
  43.2 3.2 %collective-permute-start.13 = (bf16[4,288,128]{2,1,0:T(8,128)(2,1)S(1)}, bf16[4,288,128]{2,1,0:T(8,128)(2,1)S(1)}, u32[]{:S(2)}, u32[]{:S(2)}) collective-permute-start(bf16[4,288,128]{2,1,0:T(8,128)(2,1)S(1)} %pad_maximum_fusion.2), channel_id=1, source_target_pairs={{0,8},{1,9},{2,10},{3,11},{4,12},{5,13},{6,14},{7,15},{8,0},{9,1},... | collective-permute-start | bytes 884744 | tf_op jit(solution)/shard_map/ppermute | solution.py:44
  43.3 8.1 %collective-permute-start.15 = (bf16[2,288,128]{2,1,0:T(8,128)(2,1)S(1)}, bf16[2,288,128]{2,1,0:T(8,128)(2,1)S(1)}, u32[]{:S(2)}, u32[]{:S(2)}) collective-permute-start(bf16[2,288,128]{2,1,0:T(8,128)(2,1)S(1)} %collective-permute-done.12.refs_7_.refs_4_), channel_id=1, source_target_pairs={{0,32},{1,33},{2,34},{3,35},{4,36},{5,37},{6,38},{7,39},{8,232},{9... | collective-permute-start | bytes 442376 | tf_op jit(solution)/shard_map/ppermute | solution.py:44
  43.7 7.7 %collective-permute-start.14 = (bf16[2,288,128]{2,1,0:T(8,128)(2,1)S(1)}, bf16[2,288,128]{2,1,0:T(8,128)(2,1)S(1)}, u32[]{:S(2)}, u32[]{:S(2)}) collective-permute-start(bf16[2,288,128]{2,1,0:T(8,128)(2,1)S(1)} %collective-permute-done.11.refs_6_.refs_3_), channel_id=1, source_target_pairs={{0,32},{1,33},{2,34},{3,35},{4,36},{5,37},{6,38},{7,39},{8,232},{9... | collective-permute-start | bytes 442376 | tf_op jit(solution)/shard_map/ppermute | solution.py:44
where the time goes:
time: 58.5 us; the launch traced here: 58.2 us
  Pallas kernels  19.9 us (34%)
  starting transfers between devices  17.7 us (30%)
  waiting for transfers between devices  15.1 us (26%)
  other arithmetic  2.58 us (4%)
  local copies, waits for them, and re-layouts  2.35 us (4%)
  between operations  0.62 us (1%)
    pallas_call x4, Pallas kernels, propagate(): pl.pallas_call(functools.partial(body, call, holders), out_shape=shapes,...  19.9 us
    ppermute x16, starting transfers between devices, send(): return lax.ppermute(value, BOTH, pairs)  17.7 us
    ppermute x16, waiting for transfers between devices, send(): return lax.ppermute(value, BOTH, pairs)  15.1 us
    unnamed x19, local copies, waits for them, and re-layouts  1.73 us
    select_n x4, other arithmetic, per_device(): jnp.where(keep, jnp.asarray(row_weights(s), jnp.bfloat16), 0)  1.38 us
  transfers between devices with their start and end apart: 16, of which 7 were waited for; matrix products, arithmetic and copies ran while one was open for 5% of the time, Pallas kernels for 23%

commit v1 on v0

--- a/solution.py
+++ b/solution.py
@@ -91,13 +91,13 @@
 
 
 def polynomial(func, degree):
-    w = 0.125 * (1.0 + np.cos(np.pi * (np.arange(64) + 0.5) / 64))
-    fit = np.polynomial.chebyshev.Chebyshev.fit(w, func(3.0 * np.sqrt(w)), degree, domain=[0.0, 0.25])
+    w = 0.5 * (1.0 + np.cos(np.pi * (np.arange(64) + 0.5) / 64))
+    fit = np.polynomial.chebyshev.Chebyshev.fit(w, func(1.5 * np.sqrt(w)), degree, domain=[0.0, 1.0])
     return [float(c) for c in fit.convert(kind=np.polynomial.Polynomial).coef]
 
 
-EVEN = polynomial(np.cos, 4)
-ODD = polynomial(lambda x: np.sin(x) / (x / 3.0), 4)
+EVEN = polynomial(lambda x: math.sqrt(2.0) * np.cos(x), 4)
+ODD = polynomial(lambda x: math.sqrt(2.0) * np.sin(x) / (x / 1.5), 4)
 
 
 def horner(coefs, w):
@@ -108,11 +108,9 @@
 
 
 def cosine_sine(tile):
-    v = tile - 0.5
-    w = v * v
-    cos_v, sin_v = horner(EVEN, w), horner(ODD, w) * v
-    c, s = math.cos(1.5), math.sin(1.5)
-    return cos_v * c - sin_v * s, cos_v * s + sin_v * c
+    w = tile * tile
+    c, s = horner(EVEN, w), horner(ODD, w) * tile
+    return 1.0 - s * s, s * c
 
 
 ROUNDS = (1, 2, 3, 4)
@@ -227,15 +225,17 @@
         b = plane_block(e)
         for ref, index, side in parts_of(e):
             t_re, t_im = cosine_sine(ref[index, 0 : HALF[0], :].astype(jnp.float32))
+            t_re, t_im = t_re.astype(jnp.bfloat16), t_im.astype(jnp.bfloat16)
             for wv in range(2):
                 rows = pl.ds(pl.multiple_of(side * HALF[0], 16), HALF[0])
                 x_re, x_im = x_wave[b, wv, 0:1, :], x_wave[b, wv, 1:2, :]
                 y_re, y_im = y_wave[wv, 0, rows, :], y_wave[wv, 1, rows, :]
-                re, im = x_re * y_re - x_im * y_im, x_re * y_im + x_im * y_re
+                re = (x_re * y_re - x_im * y_im).astype(jnp.bfloat16)
+                im = (x_re * y_im + x_im * y_re).astype(jnp.bfloat16)
                 rows = pl.ds(pl.multiple_of(wv * IN_ROWS[0] + side * HALF[0], 16), HALF[0])
                 for target in (fields[0].at[at], *kept):
-                    target[rows, 0:LANES] = (re * t_re - im * t_im).astype(jnp.bfloat16)
-                    target[rows, LANES:] = (re * t_im + im * t_re).astype(jnp.bfloat16)
+                    target[rows, 0:LANES] = re * t_re - im * t_im
+                    target[rows, LANES:] = re * t_im + im * t_re
     for s in range(1, SLICES):
         for e, at in trans_of(call, s).items():
             for ref, index, side in parts_of(e):
@@ -266,8 +266,9 @@
                 im = full[rows_out:, wv * LANES : (wv + 1) * LANES]
                 if s + 1 < SLICES:
                     t = trans[s].at[trans_of(call, s + 1)[e]]
-                    t_re, t_im = t[:, :LANES].astype(jnp.float32), t[:, LANES:].astype(jnp.float32)
-                    re, im = (re * t_re - im * t_im).astype(jnp.bfloat16), (re * t_im + im * t_re).astype(jnp.bfloat16)
+                    t_re, t_im = t[:, :LANES], t[:, LANES:]
+                    re, im = re.astype(jnp.bfloat16), im.astype(jnp.bfloat16)
+                    re, im = re * t_re - im * t_im, re * t_im + im * t_re
                     rows = slice(wv * rows_out, (wv + 1) * rows_out)
                     targets = [fields[s + 1].at[slots[s + 1][e]]] if e in slots[s + 1] else []
                     if not last:
@@ -357,6 +358,8 @@
     calls = []
     for k in range(1, ZS // 2 + 1):
         mine, other = send(mine, to_next), send(other, to_next)
+        if k == 1:
+            mine, other, *constants = lax.optimization_barrier((mine, other, *constants))
         if calls and k < ZS // 2:
             mine, other, _ = lax.optimization_barrier((mine, other, calls[-1][0]))
         held[((-k, True),)], held[((-k, False),)] = mine, other

time: 58.5 us -> 57.8 us (0.988)
  Pallas kernels: 19.9 us -> 18.1 us
  waiting for transfers between devices: 15.1 us -> 16.4 us
    pallas_call x4, Pallas kernels: 19.9 us -> 18.1 us  [propagate(): pl.pallas_call(functools.partial(body, call, holders), out_shape=shapes,...]
    ppermute x16, waiting for transfers between devices: 15.1 us -> 16.4 us  [send(): return lax.ppermute(value, BOTH, pairs)]
  transfers between devices with their start and end apart: 16 -> 16, of which waited for: 7 -> 9; matrix products, arithmetic and copies ran while one was open for 5% -> 5% of each run, Pallas kernels for 23% -> 21%
where the time goes in v1:
time: 57.8 us; the launch traced here: 57.6 us
  Pallas kernels  18.1 us (31%)
  starting transfers between devices  17.6 us (30%)
  waiting for transfers between devices  16.4 us (28%)
  other arithmetic  2.59 us (4%)
  local copies, waits for them, and re-layouts  2.34 us (4%)
    pallas_call x4, Pallas kernels, propagate(): pl.pallas_call(functools.partial(body, call, holders), out_shape=shapes,...  18.1 us
    ppermute x16, starting transfers between devices, send(): return lax.ppermute(value, BOTH, pairs)  17.6 us
    ppermute x16, waiting for transfers between devices, send(): return lax.ppermute(value, BOTH, pairs)  16.4 us
    unnamed x19, local copies, waits for them, and re-layouts  1.72 us
    select_n x4, other arithmetic, per_device(): jnp.where(keep, jnp.asarray(row_weights(s), jnp.bfloat16), 0)  1.38 us
  transfers between devices with their start and end apart: 16, of which 9 were waited for; matrix products, arithmetic and copies ran while one was open for 5% of the time, Pallas kernels for 21%

profile of v1, /device:TPU:16, one launch (start us, length us, event | category | flops | bytes accessed | tf_op | source)
XLA Modules:
  0.0 57.6 jit_solution(4844521577134876578)
XLA Ops:
  0.0 1.5 %collective-permute-start.1 = (bf16[4,64,64]{2,1,0:T(8,128)(2,1)}, bf16[4,64,64]{2,1,0:T(8,128)(2,1)S(1)}, u32[]{:S(2)}, u32[]{:S(2)}) collective-permute-start(bf16[4,64,64]{2,1,0:T(8,128)(2,1)} %param.7), channel_id=1, source_target_pairs={{0,16},{1,17},{2,18},{3,19},{4,20},{5,21},{6,22},{7,23},{8,24},{9,... | collective-permute-start | bytes 98312 | tf_op jit(solution)/shard_map/ppermute | solution.py:44
  1.5 0.0 collective-permute-start
  1.6 0.1 broadcast_in_dim.66
  1.7 0.1 broadcast_in_dim.72
  1.8 0.1 broadcast_in_dim.75
  1.9 0.0 copy-start.1
  1.9 1.1 %broadcast_select_fusion.refs_6_.refs_9_.refs_10_ = bf16[320,384]{1,0:T(8,128)(2,1)S(1)} fusion(bf16[320,384]{1,0:T(8,128)(2,1)} %constant.123.clone, pred[320]{0:T(512)(128)(4,1)S(1)} %broadcast_in_dim.66), kind=kLoop, calls=%fused_computation.27 | loop fusion | flops 122880 | bytes 491840 | tf_op jit(solution)/shard_map/jit(_where)/select_n | solution.py:353
  3.0 0.0 copy-done.1
  3.0 0.0 copy-start.2
  3.0 0.1 broadcast_select_fusion.1.refs_7_.refs_10_.refs_11_
  3.1 0.8 %copy-done.2 = bf16[192,256]{1,0:T(8,128)(2,1)S(1)} copy-done((bf16[192,256]{1,0:T(8,128)(2,1)S(1)}, bf16[192,256]{1,0:T(8,128)(2,1)}, u32[]{:S(2)}) %copy-start.2) | copy-done | bytes 98328
  3.9 0.0 copy-start.3
  3.9 0.1 broadcast_select_fusion.3.refs_8_.refs_11_.refs_12_
  4.0 0.7 %copy-done.3 = bf16[128,192]{1,0:T(8,128)(2,1)S(1)} copy-done((bf16[128,192]{1,0:T(8,128)(2,1)S(1)}, bf16[128,192]{1,0:T(8,128)(2,1)}, u32[]{:S(2)}) %copy-start.3) | copy-done | bytes 49176
  4.7 0.0 copy-start.4
  4.7 0.1 broadcast_select_fusion.4.refs_9_.refs_12_.refs_13_
  4.8 0.0 collective-permute-done.1
  4.8 0.6 %collective-permute-start.2 = (bf16[4,64,64]{2,1,0:T(8,128)(2,1)S(1)}, bf16[4,64,64]{2,1,0:T(8,128)(2,1)S(1)}, u32[]{:S(2)}, u32[]{:S(2)}) collective-permute-start(bf16[4,64,64]{2,1,0:T(8,128)(2,1)S(1)} %collective-permute-done.1), channel_id=1, source_target_pairs={{0,8},{1,9},{2,10},{3,11},{4,12},{5,13},{6,14},{7,15},{8,0},{9,1},... | collective-permute-start | bytes 98312 | tf_op jit(solution)/shard_map/ppermute | solution.py:44
  5.4 0.0 collective-permute-done
  5.4 0.1 copy-done.4
  5.6 0.8 %collective-permute-done.2 = bf16[4,64,64]{2,1,0:T(8,128)(2,1)S(1)} collective-permute-done((bf16[4,64,64]{2,1,0:T(8,128)(2,1)S(1)}, bf16[4,64,64]{2,1,0:T(8,128)(2,1)S(1)}, u32[]{:S(2)}, u32[]{:S(2)}) %collective-permute-start.2) | collective-permute-done | bytes 32800 | tf_op jit(solution)/shard_map/ppermute | solution.py:44
  6.4 0.1 maximum_bitcast_fusion
  6.6 4.6 %collective-permute-start.3 = (bf16[2,160,128]{2,1,0:T(8,128)(2,1)S(1)}, bf16[2,160,128]{2,1,0:T(8,128)(2,1)S(1)}, u32[]{:S(2)}, u32[]{:S(2)}) collective-permute-start(bf16[2,160,128]{2,1,0:T(8,128)(2,1)S(1)} %fusion.2), channel_id=1, source_target_pairs={{0,1},{1,2},{2,3},{3,4},{4,5},{5,6},{6,7},{9,8},{10,9},{11,10},{12... | collective-permute-start | bytes 245768 | tf_op jit(solution)/shard_map/ppermute | solution.py:44
  11.2 4.1 %collective-permute-done.3 = bf16[2,160,128]{2,1,0:T(8,128)(2,1)S(1)} collective-permute-done((bf16[2,160,128]{2,1,0:T(8,128)(2,1)S(1)}, bf16[2,160,128]{2,1,0:T(8,128)(2,1)S(1)}, u32[]{:S(2)}, u32[]{:S(2)}) %collective-permute-start.3) | collective-permute-done | bytes 81952 | tf_op jit(solution)/shard_map/ppermute | solution.py:44
  15.5 0.0 copy-start.5
  15.5 0.1 collective-permute-start.5
  15.6 2.0 %collective-permute-start.4 = (bf16[2,288,128]{2,1,0:T(8,128)(2,1)S(1)}, bf16[2,288,128]{2,1,0:T(8,128)(2,1)S(1)}, u32[]{:S(2)}, u32[]{:S(2)}) collective-permute-start(bf16[2,288,128]{2,1,0:T(8,128)(2,1)S(1)} %broadcast_select_fusion.2.refs_0_), channel_id=1, source_target_pairs={{0,32},{1,33},{2,34},{3,35},{4,36},{5,37},{6,38},{7,39},{8,232},{9... | collective-permute-start | bytes 442376 | tf_op jit(solution)/shard_map/ppermute | solution.py:44
  17.6 0.0 copy-done.5
  17.6 0.2 slice_reduce_fusion
  17.8 0.1 fusion.18
  17.9 0.5 fusion.31
  18.4 0.2 cosine_multiply_fusion
  18.5 0.0 collective-permute-done.5.refs_1_
  18.5 2.0 %collective-permute-start.6 = (bf16[2,288,128]{2,1,0:T(8,128)(2,1)S(1)}, bf16[2,288,128]{2,1,0:T(8,128)(2,1)S(1)}, u32[]{:S(2)}, u32[]{:S(2)}) collective-permute-start(bf16[2,288,128]{2,1,0:T(8,128)(2,1)S(1)} %collective-permute-done.5.refs_1_), channel_id=1, source_target_pairs={{0,32},{1,33},{2,34},{3,35},{4,36},{5,37},{6,38},{7,39},{8,232},{9... | collective-permute-start | bytes 442376 | tf_op jit(solution)/shard_map/ppermute | solution.py:44
  20.6 4.1 %collective-permute-done.4.refs_2_.refs_0_ = bf16[2,288,128]{2,1,0:T(8,128)(2,1)S(1)} collective-permute-done((bf16[2,288,128]{2,1,0:T(8,128)(2,1)S(1)}, bf16[2,288,128]{2,1,0:T(8,128)(2,1)S(1)}, u32[]{:S(2)}, u32[]{:S(2)}) %collective-permute-start.4) | collective-permute-done | bytes 147488 | tf_op jit(solution)/shard_map/ppermute | solution.py:44
  24.7 1.6 %collective-permute-done.6.refs_3_.refs_1_ = bf16[2,288,128]{2,1,0:T(8,128)(2,1)S(1)} collective-permute-done((bf16[2,288,128]{2,1,0:T(8,128)(2,1)S(1)}, bf16[2,288,128]{2,1,0:T(8,128)(2,1)S(1)}, u32[]{:S(2)}, u32[]{:S(2)}) %collective-permute-start.6) | collective-permute-done | bytes 147488 | tf_op jit(solution)/shard_map/ppermute | solution.py:44
  26.2 0.2 broadcast_in_dim.78.refs_11_.refs_14_.refs_15_
  26.4 0.0 copy-start
  26.5 0.5 collective-permute-start.9
  27.0 0.1 pad_add_fusion.where_ref
  27.0 0.0 collective-permute-start.7
  27.1 1.6 %collective-permute-start.8 = (bf16[2,288,128]{2,1,0:T(8,128)(2,1)S(1)}, bf16[2,288,128]{2,1,0:T(8,128)(2,1)S(1)}, u32[]{:S(2)}, u32[]{:S(2)}) collective-permute-start(bf16[2,288,128]{2,1,0:T(8,128)(2,1)S(1)} %collective-permute-done.6.refs_3_.refs_1_), channel_id=1, source_target_pairs={{0,32},{1,33},{2,34},{3,35},{4,36},{5,37},{6,38},{7,39},{8,232},{9... | collective-permute-start | bytes 442376 | tf_op jit(solution)/shard_map/ppermute | solution.py:44
  28.7 0.0 collective-permute-done.9.refs_4_.refs_2_
  28.7 0.0 copy-done
  28.7 3.2 %shard_map.73 = (bf16[4,384,256]{2,1,0:T(8,128)(2,1)S(1)}, bf16[4,320,256]{2,1,0:T(8,128)(2,1)S(1)}, bf16[4,256,256]{2,1,0:T(8,128)(2,1)S(1)}, bf16[4,192,256]{2,1,0:T(8,128)(2,1)S(1)}) custom-call(s32[4]{0:T(128)S(1)} %pad_add_fusion.where_ref, bf16[2,288,128]{2,1,0:T(8,128)(2,1)S(1)} %broadcast_select_fusion.2.refs_0_, ...), custom_call_target="tpu_custom_call" | custom-call | flops 4000000000 | bytes 1048576 | tf_op jit(solution)/shard_map/pallas_call | solution.py:304
  31.9 1.5 %collective-permute-done.7.refs_5_.refs_3_.refs_0_ = bf16[2,288,128]{2,1,0:T(8,128)(2,1)S(1)} collective-permute-done((bf16[2,288,128]{2,1,0:T(8,128)(2,1)S(1)}, bf16[2,288,128]{2,1,0:T(8,128)(2,1)S(1)}, u32[]{:S(2)}, u32[]{:S(2)}) %collective-permute-start.7) | collective-permute-done | bytes 147488 | tf_op jit(solution)/shard_map/ppermute | solution.py:44
  33.4 1.6 %collective-permute-done.8.refs_6_.refs_4_.refs_1_ = bf16[2,288,128]{2,1,0:T(8,128)(2,1)S(1)} collective-permute-done((bf16[2,288,128]{2,1,0:T(8,128)(2,1)S(1)}, bf16[2,288,128]{2,1,0:T(8,128)(2,1)S(1)}, u32[]{:S(2)}, u32[]{:S(2)}) %collective-permute-start.8) | collective-permute-done | bytes 147488 | tf_op jit(solution)/shard_map/ppermute | solution.py:44
  35.0 0.1 collective-permute-start.10
  35.1 0.1 collective-permute-start.11
  35.2 1.6 %collective-permute-start.12 = (bf16[2,288,128]{2,1,0:T(8,128)(2,1)S(1)}, bf16[2,288,128]{2,1,0:T(8,128)(2,1)S(1)}, u32[]{:S(2)}, u32[]{:S(2)}) collective-permute-start(bf16[2,288,128]{2,1,0:T(8,128)(2,1)S(1)} %collective-permute-done.8.refs_6_.refs_4_.refs_1_), channel_id=1, source_target_pairs={{0,32},{1,33},{2,34},{3,35},{4,36},{5,37},{6,38},{7,39},{8,232},{9... | collective-permute-start | bytes 442376 | tf_op jit(solution)/shard_map/ppermute | solution.py:44
  36.8 0.0 collective-permute-done.10.refs_7_.refs_5_.refs_2_
  36.8 4.3 %shard_map.74 = (bf16[4,384,256]{2,1,0:T(8,128)(2,1)S(1)}, bf16[4,320,256]{2,1,0:T(8,128)(2,1)S(1)}, bf16[4,256,256]{2,1,0:T(8,128)(2,1)S(1)}, bf16[4,192,256]{2...) custom-call(s32[4]{0:T(128)S(1)} %pad_add_fusion.where_ref, bf16[2,288,128]{2,1,0:T(8,128)(2,1)S(1)} %broadcast_select_fusion.2.refs_0_, ...), custom_call_target="tpu_custom_call" | custom-call | flops 7000000000 | bytes 1048576 | tf_op jit(solution)/shard_map/pallas_call | solution.py:304
  41.1 0.4 collective-permute-done.11.refs_6_.refs_3_
  41.6 1.6 %collective-permute-done.12.refs_7_.refs_4_ = bf16[2,288,128]{2,1,0:T(8,128)(2,1)S(1)} collective-permute-done((bf16[2,288,128]{2,1,0:T(8,128)(2,1)S(1)}, bf16[2,288,128]{2,1,0:T(8,128)(2,1)S(1)}, u32[]{:S(2)}, u32[]{:S(2)}) %collective-permute-start.12) | collective-permute-done | bytes 147488 | tf_op jit(solution)/shard_map/ppermute | solution.py:44
  43.2 0.1 collective-permute-start.13
  43.3 0.1 collective-permute-start.15
  43.4 2.7 %collective-permute-start.14 = (bf16[2,288,128]{2,1,0:T(8,128)(2,1)S(1)}, bf16[2,288,128]{2,1,0:T(8,128)(2,1)S(1)}, u32[]{:S(2)}, u32[]{:S(2)}) collective-permute-start(bf16[2,288,128]{2,1,0:T(8,128)(2,1)S(1)} %collective-permute-done.11.refs_6_.refs_3_), channel_id=1, source_target_pairs={{0,32},{1,33},{2,34},{3,35},{4,36},{5,37},{6,38},{7,39},{8,232},{9... | collective-permute-start | bytes 442376 | tf_op jit(solution)/shard_map/ppermute | solution.py:44
  46.1 0.0 collective-permute-done.13.refs_8_.refs_5_
  46.1 4.4 %shard_map.75 = (bf16[4,384,256]{2,1,0:T(8,128)(2,1)S(1)}, bf16[4,320,256]{2,1,0:T(8,128)(2,1)S(1)}, bf16[4,256,256]{2,1,0:T(8,128)(2,1)S(1)}, bf16[4,192,256]{2...) custom-call(s32[4]{0:T(128)S(1)} %pad_add_fusion.where_ref, ...), custom_call_target="tpu_custom_call" | custom-call | flops 7000000000 | bytes 1048576 | tf_op jit(solution)/shard_map/pallas_call | solution.py:304
  50.5 0.0 collective-permute-done.15.refs_7_
  50.6 0.7 %collective-permute-done.14.refs_6_ = bf16[2,288,128]{2,1,0:T(8,128)(2,1)S(1)} collective-permute-done((bf16[2,288,128]{2,1,0:T(8,128)(2,1)S(1)}, bf16[2,288,128]{2,1,0:T(8,128)(2,1)S(1)}, u32[]{:S(2)}, u32[]{:S(2)}) %collective-permute-start.14) | collective-permute-done | bytes 147488 | tf_op jit(solution)/shard_map/ppermute | solution.py:44
  51.3 6.1 %shard_map.76 = bf16[2,2,64,2048]{3,2,1,0:T(8,128)(2,1)} custom-call(s32[4]{0:T(128)S(1)} %pad_add_fusion.where_ref, bf16[2,288,128]{2,1,0:T(8,128)(2,1)S(1)} %collective-permute-done.7.refs_5_.refs_3_.refs_0_, bf16[2,288,128]{2,1,0:T(8,128)(2,1)S(1)} %collective-permute-done.8.refs_6_.refs_4_.refs_1_, ...), custom_call_target="tpu_custom_call" | custom-call | flops 7000000000 | bytes 1048576 | tf_op jit(solution)/shard_map/pallas_call | solution.py:304
  (37 shorter events, 0.4 us)
Async XLA Ops:
  0.0 4.8 %collective-permute-start.1 = (bf16[4,64,64]{2,1,0:T(8,128)(2,1)}, bf16[4,64,64]{2,1,0:T(8,128)(2,1)S(1)}, u32[]{:S(2)}, u32[]{:S(2)}) collective-permute-start(bf16[4,64,64]{2,1,0:T(8,128)(2,1)} %param.7), channel_id=1, source_target_pairs={{0,16},{1,17},{2,18},{3,19},{4,20},{5,21},{6,22},{7,23},{8,24},{9,... | collective-permute-start | bytes 98312 | tf_op jit(solution)/shard_map/ppermute | solution.py:44
  1.5 4.0 %collective-permute-start = (bf16[4,64,64]{2,1,0:T(8,128)(2,1)}, bf16[4,64,64]{2,1,0:T(8,128)(2,1)S(1)}, u32[]{:S(2)}, u32[]{:S(2)}) collective-permute-start(bf16[4,64,64]{2,1,0:T(8,128)(2,1)} %param.7), channel_id=1, source_target_pairs={{0,8},{1,9},{2,10},{3,11},{4,12},{5,13},{6,14},{7,15},{8,0},{9,1},... | collective-permute-start | bytes 98312 | tf_op jit(solution)/shard_map/ppermute | solution.py:44
  1.9 1.1 %copy-start.1 = (bf16[256,320]{1,0:T(8,128)(2,1)S(1)}, bf16[256,320]{1,0:T(8,128)(2,1)}, u32[]{:S(2)}) copy-start(bf16[256,320]{1,0:T(8,128)(2,1)} %constant.124.clone) | copy-start | bytes 491524
  3.0 0.9 %copy-start.2 = (bf16[192,256]{1,0:T(8,128)(2,1)S(1)}, bf16[192,256]{1,0:T(8,128)(2,1)}, u32[]{:S(2)}) copy-start(bf16[192,256]{1,0:T(8,128)(2,1)} %constant.125.clone) | copy-start | bytes 294916
  3.9 0.8 %copy-start.3 = (bf16[128,192]{1,0:T(8,128)(2,1)S(1)}, bf16[128,192]{1,0:T(8,128)(2,1)}, u32[]{:S(2)}) copy-start(bf16[128,192]{1,0:T(8,128)(2,1)} %constant.126.clone) | copy-start | bytes 147460
  4.7 0.8 %copy-start.4 = (bf16[4,64,64]{2,1,0:T(8,128)(2,1)S(1)}, bf16[4,64,64]{2,1,0:T(8,128)(2,1)}, u32[]{:S(2)}) copy-start(bf16[4,64,64]{2,1,0:T(8,128)(2,1)} %param.7) | copy-start | bytes 98308
  4.8 1.5 %collective-permute-start.2 = (bf16[4,64,64]{2,1,0:T(8,128)(2,1)S(1)}, bf16[4,64,64]{2,1,0:T(8,128)(2,1)S(1)}, u32[]{:S(2)}, u32[]{:S(2)}) collective-permute-start(bf16[4,64,64]{2,1,0:T(8,128)(2,1)S(1)} %collective-permute-done.1), channel_id=1, source_target_pairs={{0,8},{1,9},{2,10},{3,11},{4,12},{5,13},{6,14},{7,15},{8,0},{9,1},... | collective-permute-start | bytes 98312 | tf_op jit(solution)/shard_map/ppermute | solution.py:44
  6.6 8.7 %collective-permute-start.3 = (bf16[2,160,128]{2,1,0:T(8,128)(2,1)S(1)}, bf16[2,160,128]{2,1,0:T(8,128)(2,1)S(1)}, u32[]{:S(2)}, u32[]{:S(2)}) collective-permute-start(bf16[2,160,128]{2,1,0:T(8,128)(2,1)S(1)} %fusion.2), channel_id=1, source_target_pairs={{0,1},{1,2},{2,3},{3,4},{4,5},{5,6},{6,7},{9,8},{10,9},{11,10},{12... | collective-permute-start | bytes 245768 | tf_op jit(solution)/shard_map/ppermute | solution.py:44
  15.5 2.1 %copy-start.5 = (s32[2,2]{1,0:T(2,128)S(1)}, s32[2,2]{1,0:T(2,128)}, u32[]{:S(2)}) copy-start(s32[2,2]{1,0:T(2,128)} %param.8) | copy-start | bytes 52
  15.5 3.0 %collective-permute-start.5 = (bf16[2,288,128]{2,1,0:T(8,128)(2,1)S(1)}, bf16[2,288,128]{2,1,0:T(8,128)(2,1)S(1)}, u32[]{:S(2)}, u32[]{:S(2)}) collective-permute-start(bf16[2,288,128]{2,1,0:T(8,128)(2,1)S(1)} %broadcast_select_fusion.2.refs_0_), channel_id=1, source_target_pairs={{0,8},{1,9},{2,10},{3,11},{4,12},{5,13},{6,14},{7,15},{8,0},{9,1},... | collective-permute-start | bytes 442376 | tf_op jit(solution)/shard_map/ppermute | solution.py:44
  15.6 9.1 %collective-permute-start.4 = (bf16[2,288,128]{2,1,0:T(8,128)(2,1)S(1)}, bf16[2,288,128]{2,1,0:T(8,128)(2,1)S(1)}, u32[]{:S(2)}, u32[]{:S(2)}) collective-permute-start(bf16[2,288,128]{2,1,0:T(8,128)(2,1)S(1)} %broadcast_select_fusion.2.refs_0_), channel_id=1, source_target_pairs={{0,32},{1,33},{2,34},{3,35},{4,36},{5,37},{6,38},{7,39},{8,232},{9... | collective-permute-start | bytes 442376 | tf_op jit(solution)/shard_map/ppermute | solution.py:44
  18.5 7.7 %collective-permute-start.6 = (bf16[2,288,128]{2,1,0:T(8,128)(2,1)S(1)}, bf16[2,288,128]{2,1,0:T(8,128)(2,1)S(1)}, u32[]{:S(2)}, u32[]{:S(2)}) collective-permute-start(bf16[2,288,128]{2,1,0:T(8,128)(2,1)S(1)} %collective-permute-done.5.refs_1_), channel_id=1, source_target_pairs={{0,32},{1,33},{2,34},{3,35},{4,36},{5,37},{6,38},{7,39},{8,232},{9... | collective-permute-start | bytes 442376 | tf_op jit(solution)/shard_map/ppermute | solution.py:44
  26.4 2.3 %copy-start = (bf16[512,256]{1,0:T(8,128)(2,1)S(1)}, bf16[512,256]{1,0:T(8,128)(2,1)}, u32[]{:S(2)}) copy-start(bf16[512,256]{1,0:T(8,128)(2,1)} %constant.122.clone.refs_5_.refs_8_.refs_9_) | copy-start | bytes 786436
  26.5 2.2 %collective-permute-start.9 = (bf16[4,288,128]{2,1,0:T(8,128)(2,1)S(1)}, bf16[4,288,128]{2,1,0:T(8,128)(2,1)S(1)}, u32[]{:S(2)}, u32[]{:S(2)}) collective-permute-start(bf16[4,288,128]{2,1,0:T(8,128)(2,1)S(1)} %pad_maximum_fusion), channel_id=1, source_target_pairs={{0,8},{1,9},{2,10},{3,11},{4,12},{5,13},{6,14},{7,15},{8,0},{9,1},... | collective-permute-start | bytes 884744 | tf_op jit(solution)/shard_map/ppermute | solution.py:44
  27.0 6.4 %collective-permute-start.7 = (bf16[2,288,128]{2,1,0:T(8,128)(2,1)S(1)}, bf16[2,288,128]{2,1,0:T(8,128)(2,1)S(1)}, u32[]{:S(2)}, u32[]{:S(2)}) collective-permute-start(bf16[2,288,128]{2,1,0:T(8,128)(2,1)S(1)} %collective-permute-done.4.refs_2_.refs_0_), channel_id=1, source_target_pairs={{0,32},{1,33},{2,34},{3,35},{4,36},{5,37},{6,38},{7,39},{8,232},{9... | collective-permute-start | bytes 442376 | tf_op jit(solution)/shard_map/ppermute | solution.py:44
  27.1 7.9 %collective-permute-start.8 = (bf16[2,288,128]{2,1,0:T(8,128)(2,1)S(1)}, bf16[2,288,128]{2,1,0:T(8,128)(2,1)S(1)}, u32[]{:S(2)}, u32[]{:S(2)}) collective-permute-start(bf16[2,288,128]{2,1,0:T(8,128)(2,1)S(1)} %collective-permute-done.6.refs_3_.refs_1_), channel_id=1, source_target_pairs={{0,32},{1,33},{2,34},{3,35},{4,36},{5,37},{6,38},{7,39},{8,232},{9... | collective-permute-start | bytes 442376 | tf_op jit(solution)/shard_map/ppermute | solution.py:44
  35.0 1.8 %collective-permute-start.10 = (bf16[4,288,128]{2,1,0:T(8,128)(2,1)S(1)}, bf16[4,288,128]{2,1,0:T(8,128)(2,1)S(1)}, u32[]{:S(2)}, u32[]{:S(2)}) collective-permute-start(bf16[4,288,128]{2,1,0:T(8,128)(2,1)S(1)} %pad_maximum_fusion.1), channel_id=1, source_target_pairs={{0,8},{1,9},{2,10},{3,11},{4,12},{5,13},{6,14},{7,15},{8,0},{9,1},... | collective-permute-start | bytes 884744 | tf_op jit(solution)/shard_map/ppermute | solution.py:44
  35.1 6.4 %collective-permute-start.11 = (bf16[2,288,128]{2,1,0:T(8,128)(2,1)S(1)}, bf16[2,288,128]{2,1,0:T(8,128)(2,1)S(1)}, u32[]{:S(2)}, u32[]{:S(2)}) collective-permute-start(bf16[2,288,128]{2,1,0:T(8,128)(2,1)S(1)} %collective-permute-done.7.refs_5_.refs_3_.refs_0_), channel_id=1, source_target_pairs={{0,32},{1,33},{2,34},{3,35},{4,36},{5,37},{6,38},{7,39},{8,232},{9... | collective-permute-start | bytes 442376 | tf_op jit(solution)/shard_map/ppermute | solution.py:44
  35.2 7.9 %collective-permute-start.12 = (bf16[2,288,128]{2,1,0:T(8,128)(2,1)S(1)}, bf16[2,288,128]{2,1,0:T(8,128)(2,1)S(1)}, u32[]{:S(2)}, u32[]{:S(2)}) collective-permute-start(bf16[2,288,128]{2,1,0:T(8,128)(2,1)S(1)} %collective-permute-done.8.refs_6_.refs_4_.refs_1_), channel_id=1, source_target_pairs={{0,32},{1,33},{2,34},{3,35},{4,36},{5,37},{6,38},{7,39},{8,232},{9... | collective-permute-start | bytes 442376 | tf_op jit(solution)/shard_map/ppermute | solution.py:44
  43.2 2.9 %collective-permute-start.13 = (bf16[4,288,128]{2,1,0:T(8,128)(2,1)S(1)}, bf16[4,288,128]{2,1,0:T(8,128)(2,1)S(1)}, u32[]{:S(2)}, u32[]{:S(2)}) collective-permute-start(bf16[4,288,128]{2,1,0:T(8,128)(2,1)S(1)} %pad_maximum_fusion.2), channel_id=1, source_target_pairs={{0,8},{1,9},{2,10},{3,11},{4,12},{5,13},{6,14},{7,15},{8,0},{9,1},... | collective-permute-start | bytes 884744 | tf_op jit(solution)/shard_map/ppermute | solution.py:44
  43.3 7.3 %collective-permute-start.15 = (bf16[2,288,128]{2,1,0:T(8,128)(2,1)S(1)}, bf16[2,288,128]{2,1,0:T(8,128)(2,1)S(1)}, u32[]{:S(2)}, u32[]{:S(2)}) collective-permute-start(bf16[2,288,128]{2,1,0:T(8,128)(2,1)S(1)} %collective-permute-done.12.refs_7_.refs_4_), channel_id=1, source_target_pairs={{0,32},{1,33},{2,34},{3,35},{4,36},{5,37},{6,38},{7,39},{8,232},{9... | collective-permute-start | bytes 442376 | tf_op jit(solution)/shard_map/ppermute | solution.py:44
  43.4 7.9 %collective-permute-start.14 = (bf16[2,288,128]{2,1,0:T(8,128)(2,1)S(1)}, bf16[2,288,128]{2,1,0:T(8,128)(2,1)S(1)}, u32[]{:S(2)}, u32[]{:S(2)}) collective-permute-start(bf16[2,288,128]{2,1,0:T(8,128)(2,1)S(1)} %collective-permute-done.11.refs_6_.refs_3_), channel_id=1, source_target_pairs={{0,32},{1,33},{2,34},{3,35},{4,36},{5,37},{6,38},{7,39},{8,232},{9... | collective-permute-start | bytes 442376 | tf_op jit(solution)/shard_map/ppermute | solution.py:44
